TPU v7x, 32 devices: a whole 2x2x4 slice. The times are simulated.
32 devices in a mesh: parts: 2 (over x), aux: 16 (over z, y, core).
Axes of the slice: x: 2, y: 2, z: 4, core: 2. Of those that a mesh axis runs over, the one named last changes fastest.
Arguments:
- tiles: bfloat16 [32, 8, 8, 128, 128], P(('parts', 'aux')), parts along dimension 0, may hold values from -6 to 6
- mu_list: int32 [32, 8], P(('parts', 'aux')), parts along dimension 0, may hold values from 0 to 7
- lam_list: int32 [32, 8], P(('parts', 'aux')), parts along dimension 0, may hold values from 0 to 7
- tile_count: int32 [32], P(('parts', 'aux')), parts along dimension 0, may hold values from 1 to 8, as said below
- coeff: bfloat16 [2048, 256], P(('parts', 'aux')), parts along dimension 0, may hold values from -0.5 to 0.5
- owner: int32 [32], P('parts'), parts along dimension 0, may hold values from 0 to 15, each once
Outputs:
- exchange: float32 [2048, 1024], P(('parts', 'aux')), parts along dimension 0
There are 2 independent parts, one for each index of `parts`. A program takes and returns all parts, laid end to end along the dimension named above; each array names one. Nothing has to cross between parts.
Inputs may be any that keep to these rules, and one draw needn't show every extreme that they name: Slots from tile_count on are padding and are ignored; in every draw some shard uses all 8 slots.
All inputs are finite; a program needn't handle non-finite values.
Results may differ from a plain program's by a relative error of at most 0.00088.
Values may be sent and summed in bfloat16 or wider, within the bound.
A program may use at most 64 MiB of HBM per device.

v0:
```python
import jax
import jax.numpy as jnp
from jax import lax
from jax.sharding import PartitionSpec as P


def body(tiles, mu_list, lam_list, tile_count, coeff, owner):
    shards = lax.axis_size("aux")
    whole_coeff = lax.all_gather(coeff, "aux", axis=0, tiled=True)
    nbasis, occupied = whole_coeff.shape
    slots = tiles.shape[1]
    aux_local = tiles.shape[2]
    block = tiles.shape[3]
    nblocks = nbasis // block
    tile_rows = nbasis // shards
    picked = whole_coeff.reshape(nblocks, block, occupied)[lam_list[0]]
    live = (jnp.arange(slots) < tile_count[0]).astype(jnp.float32)
    products = jnp.einsum("tpml,tlo->tpmo", tiles[0], picked, preferred_element_type=jnp.float32)
    placing = (mu_list[0][:, None] == jnp.arange(nblocks)[None, :]).astype(jnp.float32) * live[
        :, None
    ]
    half_form = jnp.einsum(
        "tb,tpmo->pbmo", placing, products, precision=lax.Precision.HIGHEST
    ).astype(jnp.bfloat16)
    ordered = half_form.reshape(aux_local, shards, tile_rows, occupied)[:, owner].reshape(
        aux_local, nbasis, occupied
    )
    scale = 1.0 / (aux_local * shards * occupied)
    summed = lax.psum_scatter(
        jnp.einsum("prk,psk->rs", ordered, ordered, preferred_element_type=jnp.float32),
        "aux",
        scatter_dimension=0,
        tiled=True,
    )
    return summed * scale


def solution(mesh):
    return jax.shard_map(
        body,
        mesh=mesh,
        in_specs=(
            P(("parts", "aux"), None, None, None, None),
            P(("parts", "aux"), None),
            P(("parts", "aux"), None),
            P(("parts", "aux")),
            P(("parts", "aux"), None),
            P("parts"),
        ),
        out_specs=P(("parts", "aux"), None),
        check_vma=False,
    )
```

profile of v0, /device:TPU:0, one launch (start us, length us, event | category | flops | bytes accessed | tf_op | source)
XLA Modules:
  0.0 151.5 jit_solution(12048981923072878204)
XLA Ops:
  6.5 0.0 copy-start
  6.5 0.0 reduce-scatter.2.cloned.1.call-start
  6.5 24.9 %all_gather.3 = bf16[1024,256]{1,0:T(8,128)(2,1)S(1)} all-gather(bf16[64,256]{1,0:T(8,128)(2,1)} %param.10), channel_id=1, replica_groups=mesh['parts'=2,'aux'=16] {'aux'}, dimensions={0}, use_global_device_ids=true | all-gather | bytes 557056 | tf_op jit(solution)/shard_map/all_gather | solution.py:9
  31.4 0.7 fusion.7
  32.1 0.6 gather_fusion
  32.7 0.0 copy-done
  32.7 4.5 %convolution_bitcast_fusion = f32[8,8,128,256]{2,3,1,0:T(8,128)} fusion(bf16[1,8,8,128,128]{4,3,2,1,0:T(8,128)(2,1)S(1)} %copy-done, bf16[8,128,256]{2,1,0:T(8,128)(2,1)S(1)} %gather_fusion), kind=kOutput, calls=%fused_computation.3 | convolution fusion | flops 536870912 | bytes 11010048 | tf_op jit(solution)/shard_map/tpml,tlo->tpmo/dot_general | solution.py:18
  37.2 0.0 copy-start.1
  37.2 9.2 %copy.12 = f32[8,8,128,256]{3,0,2,1:T(8,128)} copy(f32[8,8,128,256]{2,3,1,0:T(8,128)} %convolution_bitcast_fusion) | data formatting | bytes 16777216 | tf_op jit(solution)/shard_map/tpml,tlo->tpmo/dot_general | solution.py:18
  47.1 0.0 copy-done.1
  47.1 9.4 %convert_bitcast_fusion = bf16[8,8,128,256]{3,1,2,0:T(8,128)(2,1)S(1)} fusion(f32[8,8,128,256]{3,0,2,1:T(8,128)} %copy.12, f32[8]{0:T(128)S(1)} %compare_convert_fusion, s32[8]{0:T(128)S(1)} %bitcast.37), kind=kOutput, calls=%fused_computation.2 | convolution fusion | flops 203423872 | bytes 12582976 | tf_op jit(solution)/shard_map/tb,tpmo->pbmo/dot_general | solution.py:22
  56.6 0.0 copy-start.2
  56.6 3.0 %copy.13 = bf16[8,8,128,256]{3,2,1,0:T(8,128)(2,1)} copy(bf16[8,8,128,256]{3,1,2,0:T(8,128)(2,1)S(1)} %convert_bitcast_fusion) | data formatting | bytes 8388608 | tf_op jit(solution)/shard_map/convert_element_type | solution.py:24
  59.6 0.0 copy-done.2
  59.6 5.0 %gather_fusion.1 = bf16[16,8,64,256]{3,2,1,0:T(8,128)(2,1)} fusion(bf16[8,16,64,256]{3,2,1,0:T(8,128)(2,1)} %bitcast.33, s32[1024]{0:T(1024)S(1)} %pad_clamp_fusion), kind=kCustom, calls=%fused_computation.1 | custom fusion | bytes 8388672 | tf_op jit(solution)/shard_map/gather | solution.py:25
  64.6 2.5 %copy.14 = bf16[8,16,64,256]{3,2,1,0:T(8,128)(2,1)S(1)} copy(bf16[8,16,64,256]{3,2,0,1:T(8,128)(2,1)} %bitcast.34) | data formatting | bytes 8388608 | tf_op jit(solution)/shard_map/gather | solution.py:25
  67.1 6.1 %convolution_bitcast_fusion.1 = f32[1024,1024]{1,0:T(8,128)} fusion(bf16[8,1024,256]{2,1,0:T(8,128)(2,1)S(1)} %bitcast.35), kind=kOutput, calls=%fused_computation.4 | convolution fusion | flops 4294967296 | bytes 8388608 | tf_op jit(solution)/shard_map/prk,psk->rs/dot_general | solution.py:30
  73.2 0.0 reduce-scatter.2.cloned.1.call-update
  73.2 69.8 %reduce-scatter.2.cloned.1.call-done = f32[64,1024]{1,0:T(8,128)} async-done(((f32[1024,1024]{1,0:T(8,128)}), f32[64,1024]{1,0:T(8,128)}) %reduce-scatter.2.cloned.1.call-update) | async-done | bytes 262160 | tf_op jit(solution)/shard_map/reduce_scatter | solution.py:29
  143.0 1.7 %broadcast_multiply_fusion = f32[64,1024]{1,0:T(8,128)} fusion(f32[64,1024]{1,0:T(8,128)} %reduce-scatter.2.cloned.1.call-done), kind=kLoop, calls=%fused_computation.7 | loop fusion | flops 65536 | bytes 524288 | tf_op jit(solution)/shard_map/mul | solution.py:35
  (4 shorter events, 0.0 us)
Async XLA Ops:
  6.5 26.2 %copy-start = (bf16[1,8,8,128,128]{4,3,2,1,0:T(8,128)(2,1)S(1)}, bf16[1,8,8,128,128]{4,3,2,1,0:T(8,128)(2,1)}, u32[]{:S(2)}) copy-start(bf16[1,8,8,128,128]{4,3,2,1,0:T(8,128)(2,1)} %param.6) | copy-start | bytes 6291460
  6.5 136.5 %reduce-scatter.2.cloned.1.call-start = ((), (), s32[]{:S(2)}) async-start(), calls=%async_computation.1 | async-start | bytes 4456448 | tf_op jit(solution)/shard_map/reduce_scatter | solution.py:29
  37.2 9.9 %copy-start.1 = (s32[1,8]{1,0:T(1,128)S(1)}, s32[1,8]{1,0:T(1,128)}, u32[]{:S(2)}) copy-start(s32[1,8]{1,0:T(1,128)} %param.7) | copy-start | bytes 100
  56.6 3.0 %copy-start.2 = (s32[16]{0:T(128)S(1)}, s32[16]{0:T(128)}, u32[]{:S(2)}) copy-start(s32[16]{0:T(128)} %param.11) | copy-start | bytes 196
Sparse Core Ops, SparseCore 0:
  73.3 69.6 reduce-scatter.1
where the time goes:
time: 152 us
  waiting for transfers between devices  69.8 us (46%)
  blocking collectives  24.9 us (16%)
  local copies, waits for them, and re-layouts  20.3 us (13%)
  matrix products  20.1 us (13%)
  between operations  14.1 us (9%)
  other arithmetic  2.35 us (2%)
    reduce_scatter x1, waiting for transfers between devices, body(): lax.psum_scatter(jnp.einsum('prk,psk->rs', ordered, ordered, preferred_el...  69.8 us
    all_gather x1, blocking collectives, body(): whole_coeff = lax.all_gather(coeff, 'aux', axis=0, tiled=True)  24.9 us
    dot_general x1, matrix products, body(): jnp.einsum('tb,tpmo->pbmo', placing, products, precision=lax.Precision.HI...  9.44 us
    dot_general x1, local copies, waits for them, and re-layouts, body(): jnp.einsum('tpml,tlo->tpmo', tiles[0], picked, preferred_element_type=jnp...  9.21 us
    gather x2, local copies, waits for them, and re-layouts, body(): half_form.reshape(aux_local, shards, tile_rows, occupied)[:, owner]  7.47 us
    dot_general x1, matrix products, body(): jnp.einsum('prk,psk->rs', ordered, ordered, preferred_element_type=jnp.fl...  6.09 us
    dot_general x1, matrix products, body(): jnp.einsum('tpml,tlo->tpmo', tiles[0], picked, preferred_element_type=jnp...  4.52 us
  transfers between devices with their start and end apart: 1, of which 1 were waited for; matrix products, arithmetic and copies ran while one was open for 0% of the time, Pallas kernels for 0%

commit v1 on v0

v1 whole, which is shorter than its diff:
```python
import functools

import jax
import jax.numpy as jnp
from jax import lax
from jax.experimental import pallas as pl
from jax.experimental.pallas import tpu as pltpu
from jax.sharding import PartitionSpec as P


def partial_kernel(
    shards, scale, mu_ref, lam_ref, count_ref, owner_ref, tiles_ref, coeff_ref, out_ref, half, total, place
):
    slots, aux_local, block, _ = tiles_ref.shape
    nbasis, occupied = coeff_ref.shape
    nblocks = nbasis // block
    tile_rows = nbasis // shards
    count = count_ref[0]

    @pl.loop(0, shards)
    def _(d):
        place[owner_ref[d]] = d

    @pl.loop(0, nblocks)
    def _(b):
        def add(t, seen):
            hit = (mu_ref[t] == b) & (t < count)

            def term():
                start = pl.multiple_of(lam_ref[t] * block, block)
                return jnp.dot(
                    tiles_ref[t].reshape(aux_local * block, block),
                    coeff_ref[pl.ds(start, block), :],
                    preferred_element_type=jnp.float32,
                )

            @pl.when(hit & (seen == 0))
            def _():
                total[...] = term()

            @pl.when(hit & (seen > 0))
            def _():
                total[...] += term()

            return seen + hit.astype(jnp.int32)

        seen = lax.fori_loop(0, slots, add, jnp.int32(0))
        pieces = max(block // tile_rows, 1)
        rows = block // pieces
        per_tile = tile_rows // rows
        for piece in range(pieces):
            at = b * pieces + piece
            where = pl.multiple_of(place[at // per_tile] * tile_rows + lax.rem(at, per_tile) * rows, rows)

            @pl.when(seen > 0)
            def _():
                for p in range(aux_local):
                    half[pl.ds(where, rows), p * occupied : (p + 1) * occupied] = total[
                        p * block + piece * rows : p * block + (piece + 1) * rows, :
                    ].astype(half.dtype)

            @pl.when(seen == 0)
            def _():
                half[pl.ds(where, rows), :] = jnp.zeros((rows, aux_local * occupied), half.dtype)

    chunk = 256 if nbasis % 256 == 0 else block

    @pl.loop(0, nbasis // chunk)
    def _(r):
        start = pl.multiple_of(r * chunk, chunk)
        out_ref[pl.ds(start, chunk), :] = (
            lax.dot_general(
                half[pl.ds(start, chunk), :],
                half[...],
                (((1,), (1,)), ((), ())),
                preferred_element_type=jnp.float32,
            )
            * scale
        )


def body(tiles, mu_list, lam_list, tile_count, coeff, owner):
    shards = lax.axis_size("aux")
    whole_coeff = lax.all_gather(coeff, "aux", axis=0, tiled=True)
    nbasis, occupied = whole_coeff.shape
    _, slots, aux_local, block, _ = tiles.shape
    smem = pl.BlockSpec(memory_space=pltpu.SMEM)
    vmem = pl.BlockSpec(memory_space=pltpu.VMEM)
    partial = pl.pallas_call(
        functools.partial(partial_kernel, shards, 1.0 / (aux_local * shards * occupied)),
        out_shape=jax.ShapeDtypeStruct((nbasis, nbasis), jnp.float32),
        in_specs=[smem] * 4 + [vmem] * 2,
        out_specs=vmem,
        scratch_shapes=[
            pltpu.VMEM((nbasis, aux_local * occupied), jnp.bfloat16),
            pltpu.VMEM((aux_local * block, occupied), jnp.float32),
            pltpu.SMEM((shards,), jnp.int32),
        ],
        compiler_params=pltpu.CompilerParams(vmem_limit_bytes=48 * 1024 * 1024),
    )(mu_list[0], lam_list[0], tile_count, owner, tiles[0], whole_coeff)
    return lax.psum_scatter(partial, "aux", scatter_dimension=0, tiled=True)


def solution(mesh):
    return jax.shard_map(
        body,
        mesh=mesh,
        in_specs=(
            P(("parts", "aux"), None, None, None, None),
            P(("parts", "aux"), None),
            P(("parts", "aux"), None),
            P(("parts", "aux")),
            P(("parts", "aux"), None),
            P("parts"),
        ),
        out_specs=P(("parts", "aux"), None),
        check_vma=False,
    )
```

time: 152 us -> 124 us (0.82)
  matrix products: 20.1 us -> 0 us
  local copies, waits for them, and re-layouts: 20.3 us -> 3.56 us
  Pallas kernels: 0 us -> 10.4 us
  other arithmetic: 2.35 us -> 0 us
    dot_general x3 -> x0, matrix products: 20.1 us -> none  [the longest x1 9.44 us: body(): jnp.einsum('tb,tpmo->pbmo', placing, products, precision=lax.Precision.HI...]
    pallas_call x0 -> x1, Pallas kernels: none -> 10.4 us  [body(): pl.pallas_call(functools.partial(partial_kernel, shards, 1.0 / (aux_local...]
    dot_general x1 -> x0, local copies, waits for them, and re-layouts: 9.21 us -> none  [body(): jnp.einsum('tpml,tlo->tpmo', tiles[0], picked, preferred_element_type=jnp...]
    gather x3 -> x0, local copies, waits for them, and re-layouts: 8.04 us -> none  [the longest x2 7.47 us: body(): half_form.reshape(aux_local, shards, tile_rows, occupied)[:, owner]]
    unnamed x6 -> x8, local copies, waits for them, and re-layouts: 0.01 us -> 3.56 us
    convert_element_type x1 -> x0, local copies, waits for them, and re-layouts: 3.03 us -> none  [body(): half_form = jnp.einsum('tb,tpmo->pbmo', placing, products, precision=lax....]
    mul x1 -> x0, other arithmetic: 1.67 us -> none  [body(): return summed * scale]
where the time goes in v1:
time: 124 us; the launch traced here: 123 us
  waiting for transfers between devices  70.5 us (57%)
  blocking collectives  24.8 us (20%)
  between operations  14 us (11%)
  Pallas kernels  10.4 us (8%)
  local copies, waits for them, and re-layouts  3.56 us (3%)
    reduce_scatter x1, waiting for transfers between devices, body(): return lax.psum_scatter(partial, 'aux', scatter_dimension=0, tiled=True)  70.5 us
    all_gather x1, blocking collectives, body(): whole_coeff = lax.all_gather(coeff, 'aux', axis=0, tiled=True)  24.8 us
    pallas_call x1, Pallas kernels, body(): pl.pallas_call(functools.partial(partial_kernel, shards, 1.0 / (aux_local...  10.4 us
    unnamed x8, local copies, waits for them, and re-layouts  3.56 us
  transfers between devices with their start and end apart: 1, of which 1 were waited for; matrix products, arithmetic and copies ran while one was open for 0% of the time, Pallas kernels for 0%

profile of v1, /device:TPU:0, one launch (start us, length us, event | category | flops | bytes accessed | tf_op | source)
XLA Modules:
  0.0 123.3 jit_solution(685688992027719772)
XLA Ops:
  6.5 0.0 reduce-scatter.2.cloned.1.call-start
  7.2 24.8 %all_gather.3.coeff_ref = bf16[1024,256]{1,0:T(8,128)(2,1)S(1)} all-gather(bf16[64,256]{1,0:T(8,128)(2,1)} %param.10), channel_id=1, replica_groups=mesh['parts'=2,'aux'=16] {'aux'}, dimensions={0}, use_global_device_ids=true | all-gather | bytes 557056 | tf_op jit(solution)/shard_map/all_gather | solution.py:84
  32.0 0.0 copy-start
  32.0 1.6 %copy-done = bf16[1,8,8,128,128]{4,3,2,1,0:T(8,128)(2,1)S(1)} copy-done((bf16[1,8,8,128,128]{4,3,2,1,0:T(8,128)(2,1)S(1)}, bf16[1,8,8,128,128]{4,3,2,1,0:T(8,128)(2,1)}, u32[]{:S(2)}) %copy-start) | copy-done | bytes 2097176
  33.6 0.0 copy-start.1
  33.6 0.7 copy-done.1
  34.2 0.0 copy-start.2
  34.2 0.7 copy-done.2
  34.9 0.0 copy-start.3
  34.9 0.7 copy-done.3
  35.5 10.4 %shard_map.64 = f32[1024,1024]{1,0:T(8,128)} custom-call(s32[8]{0:T(128)S(1)} %bitcast.4, s32[8]{0:T(128)S(1)} %bitcast.5, s32[1]{0:T(128)S(6)} %copy.7.count_ref, s32[16]{0:T(128)S(1)} %copy-done.3, bf16[8,8,128,128]{3,2,1,0:T(8,128)(2,1)S(1)} %bitcast.3, bf16[1024,256]{1,0:T(8,128)(2,1)S(1)} %all_gather.3.coeff_ref), custom_call_target="tpu_custom_call" | custom-call | tf_op jit(solution)/shard_map/pallas_call | solution.py:89
  46.0 0.0 reduce-scatter.2.cloned.1.call-update
  46.0 70.5 %reduce-scatter.2.cloned.1.call-done = f32[64,1024]{1,0:T(8,128)} async-done(((f32[1024,1024]{1,0:T(8,128)}), f32[64,1024]{1,0:T(8,128)}) %reduce-scatter.2.cloned.1.call-update) | async-done | bytes 262160 | tf_op jit(solution)/shard_map/reduce_scatter | solution.py:101
Async XLA Ops:
  6.5 109.9 %reduce-scatter.2.cloned.1.call-start = ((), (), s32[]{:S(2)}) async-start(), calls=%async_computation.1 | async-start | bytes 4456448 | tf_op jit(solution)/shard_map/reduce_scatter | solution.py:101
  32.0 1.6 %copy-start = (bf16[1,8,8,128,128]{4,3,2,1,0:T(8,128)(2,1)S(1)}, bf16[1,8,8,128,128]{4,3,2,1,0:T(8,128)(2,1)}, u32[]{:S(2)}) copy-start(bf16[1,8,8,128,128]{4,3,2,1,0:T(8,128)(2,1)} %param.6) | copy-start | bytes 6291460
  33.6 0.7 copy-start.1
  34.2 0.7 copy-start.2
  34.9 0.7 copy-start.3
Sparse Core Ops, SparseCore 0:
  46.1 70.2 reduce-scatter.1

commit v2 on v1

--- a/solution.py
+++ b/solution.py
@@ -7,9 +7,11 @@
 from jax.experimental.pallas import tpu as pltpu
 from jax.sharding import PartitionSpec as P
 
+MESH = pl.DeviceIdType.MESH
+
 
 def partial_kernel(
-    shards, scale, mu_ref, lam_ref, count_ref, owner_ref, tiles_ref, coeff_ref, out_ref, half, total, place
+    shards, scale, band, mu_ref, lam_ref, count_ref, owner_ref, tiles_ref, coeff_ref, out_ref, half, total, place
 ):
     slots, aux_local, block, _ = tiles_ref.shape
     nbasis, occupied = coeff_ref.shape
@@ -57,48 +59,223 @@
                 for p in range(aux_local):
                     half[pl.ds(where, rows), p * occupied : (p + 1) * occupied] = total[
                         p * block + piece * rows : p * block + (piece + 1) * rows, :
-                    ].astype(half.dtype)
+                    ].astype(jnp.bfloat16).astype(half.dtype)
 
             @pl.when(seen == 0)
             def _():
                 half[pl.ds(where, rows), :] = jnp.zeros((rows, aux_local * occupied), half.dtype)
 
-    chunk = 256 if nbasis % 256 == 0 else block
-
-    @pl.loop(0, nbasis // chunk)
-    def _(r):
-        start = pl.multiple_of(r * chunk, chunk)
-        out_ref[pl.ds(start, chunk), :] = (
-            lax.dot_general(
-                half[pl.ds(start, chunk), :],
-                half[...],
-                (((1,), (1,)), ((), ())),
-                preferred_element_type=jnp.float32,
-            )
-            * scale
-        )
+    if band:
+        half[nbasis:, :] = half[: half.shape[0] - nbasis, :]
+
+        @pl.loop(0, nblocks)
+        def _(d):
+            start = pl.multiple_of(d * block, block)
+            out_ref[d] = (
+                lax.dot_general(
+                    half[pl.ds(start, block), :],
+                    half[pl.ds(start, band), :],
+                    (((1,), (1,)), ((), ())),
+                    preferred_element_type=jnp.float32,
+                )
+                * scale
+            )
+
+    else:
+
+        @pl.loop(0, nblocks)
+        def _(d):
+            start = pl.multiple_of(d * block, block)
+            out_ref[pl.ds(start, block), :] = (
+                lax.dot_general(
+                    half[pl.ds(start, block), :].astype(jnp.bfloat16),
+                    half[...].astype(jnp.bfloat16),
+                    (((1,), (1,)), ((), ())),
+                    preferred_element_type=jnp.float32,
+                )
+                * scale
+            )
+
+
+def greet(me, shards):
+    barrier = pltpu.get_barrier_semaphore()
+    for k in range(1, shards):
+        pl.semaphore_signal(barrier, inc=1, device_id={"aux": lax.rem(me + k, shards)}, device_id_type=MESH)
+    pl.semaphore_wait(barrier, shards - 1)
+
+
+def push(src, dst, send, recv, device):
+    copy = pltpu.make_async_remote_copy(
+        src_ref=src, dst_ref=dst, send_sem=send, recv_sem=recv, device_id={"aux": device}, device_id_type=MESH
+    )
+    copy.start()
+    return copy
+
+
+def gather_kernel(shards, coeff_ref, out_ref, send, recv, pass_send, pass_recv):
+    me = lax.axis_index("aux")
+    rows = coeff_ref.shape[0]
+    chips = shards // 2
+    chip, core = me // 2, lax.rem(me, 2)
+    sibling = chip * 2 + 1 - core
+
+    def rows_of(device):
+        return out_ref.at[pl.ds(pl.multiple_of(device * rows, rows), rows), :]
+
+    greet(me, shards)
+    copies = []
+    for k in range(1, chips):
+        target = lax.rem(chip + k, chips) * 2 + core
+        copies.append(push(coeff_ref, rows_of(me), send.at[k], recv.at[k], target))
+    passed = [push(coeff_ref, rows_of(me), pass_send.at[0], pass_recv.at[0], sibling)]
+    out_ref[pl.ds(pl.multiple_of(me * rows, rows), rows), :] = coeff_ref[...]
+    for k in range(1, chips):
+        copies[k - 1].wait_recv()
+        source = lax.rem(chip + chips - k, chips) * 2 + core
+        passed.append(push(rows_of(source), rows_of(source), pass_send.at[k], pass_recv.at[k], sibling))
+    for copy in copies:
+        copy.wait_send()
+    for copy in passed:
+        copy.wait()
+
+
+def scatter_kernel(
+    shards, part_ref, out_ref, from_core, to_y, from_y, held, from_z, turned, from_far, core_s, core_r, y_s, y_r, z_s, z_r, far_s, far_r
+):
+    me = lax.axis_index("aux")
+    chips, block, band = part_ref.shape
+    rows = block // 2
+    depth = chips // 2
+    chip, core = me // 2, lax.rem(me, 2)
+    z, y = chip // 2, lax.rem(chip, 2)
+    sibling = chip * 2 + 1 - core
+    mine = pl.ds(pl.multiple_of(core * rows, rows), rows)
+    theirs = pl.ds(pl.multiple_of((1 - core) * rows, rows), rows)
+    offsets = list(range(depth // 2, 0, -1)) + list(range(depth // 2 + 1, depth)) + [0]
+
+    greet(me, shards)
+    cores = {}
+    for k in offsets:
+        for v in (1, 0):
+            d = lax.rem(z + k, depth) * 2 + (y if v == 0 else 1 - y)
+            cores[k, v] = push(
+                part_ref.at[d, theirs, :], from_core.at[2 * k + v], core_s.at[2 * k + v], core_r.at[2 * k + v], sibling
+            )
+    ys = {}
+    for k in offsets:
+        d = lax.rem(z + k, depth) * 2
+        cores[k, 1].wait_recv()
+        to_y[k] = part_ref[d + 1 - y, mine, :] + from_core[2 * k + 1]
+        ys[k] = push(to_y.at[k], from_y.at[k], y_s.at[k], y_r.at[k], (z * 2 + 1 - y) * 2 + core)
+        cores[k, 0].wait_recv()
+        held[k] = part_ref[d + y, mine, :] + from_core[2 * k]
+    zs = {}
+    for k in offsets:
+        ys[k].wait_recv()
+        held[k] += from_y[k]
+        if k:
+            zs[k] = push(held.at[k], from_z.at[k], z_s.at[k], z_r.at[k], (lax.rem(z + k, depth) * 2 + y) * 2 + core)
+    for k in zs:
+        zs[k].wait_recv()
+        held[0] += from_z[k]
+
+    fars = []
+    near = band // block
+    for k in range(1, chips - near + 1):
+        turned[k - 1] = held[0, :, k * block : (k + 1) * block].T
+        for h in range(2):
+            n = 2 * (k - 1) + h
+            fars.append(
+                push(
+                    turned.at[k - 1, h * rows : (h + 1) * rows, :],
+                    from_far.at[2 * (k - 1) + core],
+                    far_s.at[n],
+                    far_r.at[2 * (k - 1) + core],
+                    lax.rem(chip + k, chips) * 2 + h,
+                )
+            )
+    for k in range(near):
+        at = pl.multiple_of(lax.rem(chip + k, chips) * block, block)
+        out_ref[:, pl.ds(at, block)] = held[0, :, k * block : (k + 1) * block]
+    for copy in fars:
+        copy.wait_send()
+    for k in range(1, chips - near + 1):
+        for c in range(2):
+            n = 2 * (k - 1) + c
+            pltpu.make_async_copy(from_far.at[n], from_far.at[n], far_r.at[n]).wait()
+        at = pl.multiple_of(lax.rem(chip + chips - k, chips) * block, block)
+        out_ref[:, pl.ds(at, block)] = jnp.concatenate([from_far[2 * k - 2], from_far[2 * k - 1]], axis=1)
+    for group in (cores, ys, zs):
+        for copy in group.values():
+            copy.wait_send()
 
 
 def body(tiles, mu_list, lam_list, tile_count, coeff, owner):
     shards = lax.axis_size("aux")
-    whole_coeff = lax.all_gather(coeff, "aux", axis=0, tiled=True)
-    nbasis, occupied = whole_coeff.shape
+    own_rows, occupied = coeff.shape
+    nbasis = own_rows * shards
     _, slots, aux_local, block, _ = tiles.shape
+    nblocks = nbasis // block
     smem = pl.BlockSpec(memory_space=pltpu.SMEM)
     vmem = pl.BlockSpec(memory_space=pltpu.VMEM)
+    dma = pltpu.SemaphoreType.DMA
+    own = own_rows * 2 == block and nblocks % 4 == 0
+    band = (nblocks // 2 + 1) * block if own else 0
+    if own:
+        whole_coeff = pl.pallas_call(
+            functools.partial(gather_kernel, shards),
+            out_shape=jax.ShapeDtypeStruct((nbasis, occupied), coeff.dtype),
+            in_specs=[vmem],
+            out_specs=vmem,
+            scratch_shapes=[dma((nblocks,))] * 4,
+            compiler_params=pltpu.CompilerParams(collective_id=0, has_side_effects=True),
+        )(coeff)
+    else:
+        whole_coeff = lax.all_gather(coeff, "aux", axis=0, tiled=True)
+    wide = jnp.bfloat16 if own_rows % 16 == 0 else jnp.float32
     partial = pl.pallas_call(
-        functools.partial(partial_kernel, shards, 1.0 / (aux_local * shards * occupied)),
-        out_shape=jax.ShapeDtypeStruct((nbasis, nbasis), jnp.float32),
+        functools.partial(partial_kernel, shards, 1.0 / (aux_local * shards * occupied), band),
+        out_shape=jax.ShapeDtypeStruct((nblocks, block, band) if own else (nbasis, nbasis), jnp.float32),
         in_specs=[smem] * 4 + [vmem] * 2,
         out_specs=vmem,
         scratch_shapes=[
-            pltpu.VMEM((nbasis, aux_local * occupied), jnp.bfloat16),
+            pltpu.VMEM((nbasis + max(band - block, 0), aux_local * occupied), wide),
             pltpu.VMEM((aux_local * block, occupied), jnp.float32),
             pltpu.SMEM((shards,), jnp.int32),
         ],
         compiler_params=pltpu.CompilerParams(vmem_limit_bytes=48 * 1024 * 1024),
     )(mu_list[0], lam_list[0], tile_count, owner, tiles[0], whole_coeff)
-    return lax.psum_scatter(partial, "aux", scatter_dimension=0, tiled=True)
+    if not own:
+        return lax.psum_scatter(partial, "aux", scatter_dimension=0, tiled=True)
+    depth = nblocks // 2
+    far = nblocks - band // block
+    f32 = jnp.float32
+    return pl.pallas_call(
+        functools.partial(scatter_kernel, shards),
+        out_shape=jax.ShapeDtypeStruct((own_rows, nbasis), f32),
+        in_specs=[vmem],
+        out_specs=vmem,
+        scratch_shapes=[
+            pltpu.VMEM((nblocks, own_rows, band), f32),
+            pltpu.VMEM((depth, own_rows, band), f32),
+            pltpu.VMEM((depth, own_rows, band), f32),
+            pltpu.VMEM((depth, own_rows, band), f32),
+            pltpu.VMEM((depth, own_rows, band), f32),
+            pltpu.VMEM((far, block, own_rows), f32),
+            pltpu.VMEM((2 * far, own_rows, own_rows), f32),
+            dma((nblocks,)),
+            dma((nblocks,)),
+            dma((depth,)),
+            dma((depth,)),
+            dma((depth,)),
+            dma((depth,)),
+            dma((2 * far,)),
+            dma((2 * far,)),
+        ],
+        compiler_params=pltpu.CompilerParams(
+            collective_id=1, has_side_effects=True, vmem_limit_bytes=32 * 1024 * 1024
+        ),
+    )(partial)
 
 
 def solution(mesh):

time: 124 us -> 67 us (0.54)
  the two profiles are of different devices: /device:TPU:0 before, /device:TPU:27 now
where the time goes in v2:
time: 67 us; the launch traced here: 66.5 us
  Pallas kernels  60.5 us (90%)
  local copies, waits for them, and re-layouts  5.3 us (8%)
  between operations  0.69 us (1%)
    pallas_call x1, Pallas kernels, body(): pl.pallas_call(functools.partial(scatter_kernel, shards), out_shape=jax.S...  36.2 us
    pallas_call x1, Pallas kernels, body(): pl.pallas_call(functools.partial(gather_kernel, shards), out_shape=jax.Sh...  13.6 us
    pallas_call x1, Pallas kernels, body(): pl.pallas_call(functools.partial(partial_kernel, shards, 1.0 / (aux_local...  10.7 us
    unnamed x11, local copies, waits for them, and re-layouts  5.3 us

profile of v2, /device:TPU:27, one launch (start us, length us, event | category | flops | bytes accessed | tf_op | source)
XLA Modules:
  0.0 66.5 jit_solution(17195839701787947698)
XLA Ops:
  0.7 13.6 %shard_map.64.coeff_ref = bf16[1024,256]{1,0:T(8,128)(2,1)} custom-call(bf16[64,256]{1,0:T(8,128)(2,1)} %coeff_ref.1), custom_call_target="tpu_custom_call" | custom-call | tf_op jit(solution)/shard_map/pallas_call | solution.py:225
  14.2 0.0 copy-start
  14.2 1.6 %copy-done = bf16[1,8,8,128,128]{4,3,2,1,0:T(8,128)(2,1)S(1)} copy-done((bf16[1,8,8,128,128]{4,3,2,1,0:T(8,128)(2,1)S(1)}, bf16[1,8,8,128,128]{4,3,2,1,0:T(8,128)(2,1)}, u32[]{:S(2)}) %copy-start) | copy-done | bytes 2097176
  15.8 0.0 copy-start.1
  15.8 1.0 %copy-done.1 = bf16[1024,256]{1,0:T(8,128)(2,1)S(1)} copy-done((bf16[1024,256]{1,0:T(8,128)(2,1)S(1)}, bf16[1024,256]{1,0:T(8,128)(2,1)}, u32[]{:S(2)}) %copy-start.1) | copy-done | bytes 524312
  16.9 0.0 copy-start.2
  16.9 0.7 copy-done.2
  17.5 0.0 copy-start.3
  17.5 0.7 copy-done.3
  18.2 0.0 copy-start.4
  18.2 0.7 copy-done.4
  18.8 10.7 %shard_map.65.part_ref = f32[8,128,640]{2,1,0:T(8,128)S(1)} custom-call(s32[8]{0:T(128)S(1)} %bitcast.4, s32[8]{0:T(128)S(1)} %bitcast.5, s32[1]{0:T(128)S(6)} %copy.8.count_ref, s32[16]{0:T(128)S(1)} %copy-done.4, bf16[8,8,128,128]{3,2,1,0:T(8,128)(2,1)S(1)} %bitcast.3, bf16[1024,256]{1,0:T(8,128)(2,1)S(1)} %copy-done.1), custom_call_target="tpu_custom_call" | custom-call | tf_op jit(solution)/shard_map/pallas_call | solution.py:236
  29.5 36.2 %shard_map.66 = f32[64,1024]{1,0:T(8,128)S(1)} custom-call(f32[8,128,640]{2,1,0:T(8,128)S(1)} %shard_map.65.part_ref), custom_call_target="tpu_custom_call" | custom-call | tf_op jit(solution)/shard_map/pallas_call | solution.py:253
  65.8 0.7 %copy.9 = f32[64,1024]{1,0:T(8,128)} copy(f32[64,1024]{1,0:T(8,128)S(1)} %shard_map.66) | data formatting | bytes 524288
Async XLA Ops:
  14.2 1.6 %copy-start = (bf16[1,8,8,128,128]{4,3,2,1,0:T(8,128)(2,1)S(1)}, bf16[1,8,8,128,128]{4,3,2,1,0:T(8,128)(2,1)}, u32[]{:S(2)}) copy-start(bf16[1,8,8,128,128]{4,3,2,1,0:T(8,128)(2,1)} %param.6) | copy-start | bytes 6291460
  15.8 1.0 %copy-start.1 = (bf16[1024,256]{1,0:T(8,128)(2,1)S(1)}, bf16[1024,256]{1,0:T(8,128)(2,1)}, u32[]{:S(2)}) copy-start(bf16[1024,256]{1,0:T(8,128)(2,1)} %shard_map.64.coeff_ref) | copy-start | bytes 1572868
  16.9 0.7 copy-start.2
  17.5 0.7 copy-start.3
  18.2 0.7 copy-start.4

commit v3 on v2

--- a/solution.py
+++ b/solution.py
@@ -11,8 +11,26 @@
 
 
 def partial_kernel(
-    shards, scale, band, mu_ref, lam_ref, count_ref, owner_ref, tiles_ref, coeff_ref, out_ref, half, total, place
+    shards, scale, own, mu_in, lam_in, count_in, owner_in, tiles_in, coeff_ref, out_ref, *rest
 ):
+    *spare, total, tiles_ref, mu_ref, lam_ref, count_ref, owner_ref, place, sems = rest
+    half = out_ref if own else spare[0]
+    moves = [
+        pltpu.make_async_copy(src, dst, sems.at[n])
+        for n, (src, dst) in enumerate(
+            (
+                (mu_in, mu_ref),
+                (lam_in, lam_ref),
+                (count_in, count_ref),
+                (owner_in, owner_ref),
+                (tiles_in, tiles_ref),
+            )
+        )
+    ]
+    for move in moves:
+        move.start()
+    for move in moves:
+        move.wait()
     slots, aux_local, block, _ = tiles_ref.shape
     nbasis, occupied = coeff_ref.shape
     nblocks = nbasis // block
@@ -65,22 +83,8 @@
             def _():
                 half[pl.ds(where, rows), :] = jnp.zeros((rows, aux_local * occupied), half.dtype)
 
-    if band:
+    if own:
         half[nbasis:, :] = half[: half.shape[0] - nbasis, :]
-
-        @pl.loop(0, nblocks)
-        def _(d):
-            start = pl.multiple_of(d * block, block)
-            out_ref[d] = (
-                lax.dot_general(
-                    half[pl.ds(start, block), :],
-                    half[pl.ds(start, band), :],
-                    (((1,), (1,)), ((), ())),
-                    preferred_element_type=jnp.float32,
-                )
-                * scale
-            )
-
     else:
 
         @pl.loop(0, nblocks)
@@ -140,7 +144,7 @@
 
 
 def scatter_kernel(
-    shards, part_ref, out_ref, from_core, to_y, from_y, held, from_z, turned, from_far, core_s, core_r, y_s, y_r, z_s, z_r, far_s, far_r
+    shards, scale, half_ref, out_ref, part_ref, from_core, to_y, from_y, held, from_z, turned, from_far, core_s, core_r, y_s, y_r, z_s, z_r, far_s, far_r
 ):
     me = lax.axis_index("aux")
     chips, block, band = part_ref.shape
@@ -154,25 +158,42 @@
     offsets = list(range(depth // 2, 0, -1)) + list(range(depth // 2 + 1, depth)) + [0]
 
     greet(me, shards)
-    cores = {}
+    cores, ys = {}, {}
+
+    def multiply(k, v):
+        n = 2 * k + v
+        d = lax.rem(z + k, depth) * 2 + (y if v == 0 else 1 - y)
+        start = pl.multiple_of(d * block, block)
+        part_ref[n] = (
+            lax.dot_general(
+                half_ref[pl.ds(start, block), :],
+                half_ref[pl.ds(start, band), :],
+                (((1,), (1,)), ((), ())),
+                preferred_element_type=jnp.float32,
+            )
+            * scale
+        )
+        cores[k, v] = push(part_ref.at[n, theirs, :], from_core.at[n], core_s.at[n], core_r.at[n], sibling)
+
+    def send_on(k):
+        cores[k, 1].wait_recv()
+        to_y[k] = part_ref[2 * k + 1, mine, :] + from_core[2 * k + 1]
+        ys[k] = push(to_y.at[k], from_y.at[k], y_s.at[k], y_r.at[k], (z * 2 + 1 - y) * 2 + core)
+
+    before = None
     for k in offsets:
-        for v in (1, 0):
-            d = lax.rem(z + k, depth) * 2 + (y if v == 0 else 1 - y)
-            cores[k, v] = push(
-                part_ref.at[d, theirs, :], from_core.at[2 * k + v], core_s.at[2 * k + v], core_r.at[2 * k + v], sibling
-            )
-    ys = {}
+        multiply(k, 1)
+        if before is not None:
+            send_on(before)
+        before = k
+    send_on(before)
     for k in offsets:
-        d = lax.rem(z + k, depth) * 2
-        cores[k, 1].wait_recv()
-        to_y[k] = part_ref[d + 1 - y, mine, :] + from_core[2 * k + 1]
-        ys[k] = push(to_y.at[k], from_y.at[k], y_s.at[k], y_r.at[k], (z * 2 + 1 - y) * 2 + core)
-        cores[k, 0].wait_recv()
-        held[k] = part_ref[d + y, mine, :] + from_core[2 * k]
+        multiply(k, 0)
     zs = {}
     for k in offsets:
+        cores[k, 0].wait_recv()
         ys[k].wait_recv()
-        held[k] += from_y[k]
+        held[k] = part_ref[2 * k, mine, :] + from_core[2 * k] + from_y[k]
         if k:
             zs[k] = push(held.at[k], from_z.at[k], z_s.at[k], z_r.at[k], (lax.rem(z + k, depth) * 2 + y) * 2 + core)
     for k in zs:
@@ -216,7 +237,8 @@
     nbasis = own_rows * shards
     _, slots, aux_local, block, _ = tiles.shape
     nblocks = nbasis // block
-    smem = pl.BlockSpec(memory_space=pltpu.SMEM)
+    depth_of_sum = aux_local * occupied
+    scale = 1.0 / (depth_of_sum * shards)
     vmem = pl.BlockSpec(memory_space=pltpu.VMEM)
     dma = pltpu.SemaphoreType.DMA
     own = own_rows * 2 == block and nblocks % 4 == 0
@@ -224,7 +246,7 @@
     if own:
         whole_coeff = pl.pallas_call(
             functools.partial(gather_kernel, shards),
-            out_shape=jax.ShapeDtypeStruct((nbasis, occupied), coeff.dtype),
+            out_shape=pltpu.VMEM((nbasis, occupied), coeff.dtype),
             in_specs=[vmem],
             out_specs=vmem,
             scratch_shapes=[dma((nblocks,))] * 4,
@@ -234,16 +256,24 @@
         whole_coeff = lax.all_gather(coeff, "aux", axis=0, tiled=True)
     wide = jnp.bfloat16 if own_rows % 16 == 0 else jnp.float32
     partial = pl.pallas_call(
-        functools.partial(partial_kernel, shards, 1.0 / (aux_local * shards * occupied), band),
-        out_shape=jax.ShapeDtypeStruct((nblocks, block, band) if own else (nbasis, nbasis), jnp.float32),
-        in_specs=[smem] * 4 + [vmem] * 2,
+        functools.partial(partial_kernel, shards, scale, own),
+        out_shape=pltpu.VMEM((nbasis + band - block, depth_of_sum), jnp.bfloat16)
+        if own
+        else jax.ShapeDtypeStruct((nbasis, nbasis), jnp.float32),
+        in_specs=[pl.BlockSpec(memory_space=pltpu.HBM)] * 5 + [vmem],
         out_specs=vmem,
-        scratch_shapes=[
-            pltpu.VMEM((nbasis + max(band - block, 0), aux_local * occupied), wide),
+        scratch_shapes=([] if own else [pltpu.VMEM((nbasis, depth_of_sum), wide)])
+        + [
             pltpu.VMEM((aux_local * block, occupied), jnp.float32),
+            pltpu.VMEM((slots, aux_local, block, block), tiles.dtype),
+            pltpu.SMEM((slots,), jnp.int32),
+            pltpu.SMEM((slots,), jnp.int32),
+            pltpu.SMEM((1,), jnp.int32),
             pltpu.SMEM((shards,), jnp.int32),
+            pltpu.SMEM((shards,), jnp.int32),
+            dma((5,)),
         ],
-        compiler_params=pltpu.CompilerParams(vmem_limit_bytes=48 * 1024 * 1024),
+        compiler_params=pltpu.CompilerParams(vmem_limit_bytes=(56 if own else 48) * 1024 * 1024),
     )(mu_list[0], lam_list[0], tile_count, owner, tiles[0], whole_coeff)
     if not own:
         return lax.psum_scatter(partial, "aux", scatter_dimension=0, tiled=True)
@@ -251,11 +281,12 @@
     far = nblocks - band // block
     f32 = jnp.float32
     return pl.pallas_call(
-        functools.partial(scatter_kernel, shards),
+        functools.partial(scatter_kernel, shards, scale),
         out_shape=jax.ShapeDtypeStruct((own_rows, nbasis), f32),
         in_specs=[vmem],
         out_specs=vmem,
         scratch_shapes=[
+            pltpu.VMEM((nblocks, block, band), f32),
             pltpu.VMEM((nblocks, own_rows, band), f32),
             pltpu.VMEM((depth, own_rows, band), f32),
             pltpu.VMEM((depth, own_rows, band), f32),
@@ -273,7 +304,7 @@
             dma((2 * far,)),
         ],
         compiler_params=pltpu.CompilerParams(
-            collective_id=1, has_side_effects=True, vmem_limit_bytes=32 * 1024 * 1024
+            collective_id=1, has_side_effects=True, vmem_limit_bytes=24 * 1024 * 1024
         ),
     )(partial)
 

time: 67 us -> 58.8 us (0.88)
  the two profiles are of different devices: /device:TPU:27 before, /device:TPU:0 now
where the time goes in v3:
time: 58.8 us; the launch traced here: 58.9 us
  Pallas kernels  56.7 us (96%)
  local copies, waits for them, and re-layouts  1.48 us (3%)
  between operations  0.68 us (1%)
    pallas_call x1, Pallas kernels, body(): pl.pallas_call(functools.partial(scatter_kernel, shards, scale), out_shap...  38.1 us
    pallas_call x1, Pallas kernels, body(): pl.pallas_call(functools.partial(gather_kernel, shards), out_shape=pltpu....  13.3 us
    pallas_call x1, Pallas kernels, body(): pl.pallas_call(functools.partial(partial_kernel, shards, scale, own), out...  5.3 us
    unnamed x3, local copies, waits for them, and re-layouts  1.48 us

profile of v3, /device:TPU:0, one launch (start us, length us, event | category | flops | bytes accessed | tf_op | source)
XLA Modules:
  0.0 58.9 jit_solution(13796409195328292160)
XLA Ops:
  0.7 13.3 %shard_map.64.coeff_ref = bf16[1024,256]{1,0:T(8,128)(2,1)S(1)} custom-call(bf16[64,256]{1,0:T(8,128)(2,1)} %coeff_ref.1), custom_call_target="tpu_custom_call" | custom-call | tf_op jit(solution)/shard_map/pallas_call | solution.py:247
  13.9 0.0 copy-start
  13.9 0.8 %copy-done = bf16[1024,256]{1,0:T(8,128)(2,1)} copy-done((bf16[1024,256]{1,0:T(8,128)(2,1)}, bf16[1024,256]{1,0:T(8,128)(2,1)S(1)}, u32[]{:S(2)}) %copy-start) | copy-done | bytes 524312
  14.7 5.3 %shard_map.65.half_ref = bf16[1536,2048]{1,0:T(8,128)(2,1)S(1)} custom-call(s32[8]{0:T(128)} %bitcast.4, s32[8]{0:T(128)} %bitcast.5, s32[1]{0:T(128)S(6)} %copy.8.count_in, s32[16]{0:T(128)} %owner_in.1, bf16[8,8,128,128]{3,2,1,0:T(8,128)(2,1)} %bitcast.3, bf16[1024,256]{1,0:T(8,128)(2,1)} %copy-done), custom_call_target="tpu_custom_call" | custom-call | tf_op jit(solution)/shard_map/pallas_call | solution.py:258
  20.0 38.1 %shard_map.66 = f32[64,1024]{1,0:T(8,128)S(1)} custom-call(bf16[1536,2048]{1,0:T(8,128)(2,1)S(1)} %shard_map.65.half_ref), custom_call_target="tpu_custom_call" | custom-call | tf_op jit(solution)/shard_map/pallas_call | solution.py:283
  58.2 0.7 %copy.9 = f32[64,1024]{1,0:T(8,128)} copy(f32[64,1024]{1,0:T(8,128)S(1)} %shard_map.66) | data formatting | bytes 524288
Async XLA Ops:
  13.9 0.8 %copy-start = (bf16[1024,256]{1,0:T(8,128)(2,1)}, bf16[1024,256]{1,0:T(8,128)(2,1)S(1)}, u32[]{:S(2)}) copy-start(bf16[1024,256]{1,0:T(8,128)(2,1)S(1)} %shard_map.64.coeff_ref) | copy-start | bytes 1572868

commit v4 on v3

--- a/solution.py
+++ b/solution.py
@@ -105,7 +105,7 @@
     barrier = pltpu.get_barrier_semaphore()
     for k in range(1, shards):
         pl.semaphore_signal(barrier, inc=1, device_id={"aux": lax.rem(me + k, shards)}, device_id_type=MESH)
-    pl.semaphore_wait(barrier, shards - 1)
+    return lambda: pl.semaphore_wait(barrier, shards - 1)
 
 
 def push(src, dst, send, recv, device):
@@ -126,13 +126,14 @@
     def rows_of(device):
         return out_ref.at[pl.ds(pl.multiple_of(device * rows, rows), rows), :]
 
-    greet(me, shards)
+    met = greet(me, shards)
+    out_ref[pl.ds(pl.multiple_of(me * rows, rows), rows), :] = coeff_ref[...]
+    met()
     copies = []
     for k in range(1, chips):
         target = lax.rem(chip + k, chips) * 2 + core
         copies.append(push(coeff_ref, rows_of(me), send.at[k], recv.at[k], target))
     passed = [push(coeff_ref, rows_of(me), pass_send.at[0], pass_recv.at[0], sibling)]
-    out_ref[pl.ds(pl.multiple_of(me * rows, rows), rows), :] = coeff_ref[...]
     for k in range(1, chips):
         copies[k - 1].wait_recv()
         source = lax.rem(chip + chips - k, chips) * 2 + core
@@ -157,7 +158,7 @@
     theirs = pl.ds(pl.multiple_of((1 - core) * rows, rows), rows)
     offsets = list(range(depth // 2, 0, -1)) + list(range(depth // 2 + 1, depth)) + [0]
 
-    greet(me, shards)
+    met = greet(me, shards)
     cores, ys = {}, {}
 
     def multiply(k, v):
@@ -173,6 +174,8 @@
             )
             * scale
         )
+        if (k, v) == (offsets[0], 1):
+            met()
         cores[k, v] = push(part_ref.at[n, theirs, :], from_core.at[n], core_s.at[n], core_r.at[n], sibling)
 
     def send_on(k):
@@ -203,12 +206,16 @@
     fars = []
     near = band // block
     for k in range(1, chips - near + 1):
-        turned[k - 1] = held[0, :, k * block : (k + 1) * block].T
+        flipped = held[0, :, k * block : (k + 1) * block].T
         for h in range(2):
+            low = h * rows
+            turned[2 * (k - 1) + h] = jnp.concatenate(
+                [flipped[low : low + rows // 2, :], flipped[low + rows // 2 : low + rows, :]], axis=1
+            )
             n = 2 * (k - 1) + h
             fars.append(
                 push(
-                    turned.at[k - 1, h * rows : (h + 1) * rows, :],
+                    turned.at[n],
                     from_far.at[2 * (k - 1) + core],
                     far_s.at[n],
                     far_r.at[2 * (k - 1) + core],
@@ -225,7 +232,9 @@
             n = 2 * (k - 1) + c
             pltpu.make_async_copy(from_far.at[n], from_far.at[n], far_r.at[n]).wait()
         at = pl.multiple_of(lax.rem(chip + chips - k, chips) * block, block)
-        out_ref[:, pl.ds(at, block)] = jnp.concatenate([from_far[2 * k - 2], from_far[2 * k - 1]], axis=1)
+        first, second = from_far[2 * k - 2], from_far[2 * k - 1]
+        out_ref[: rows // 2, pl.ds(at, block)] = jnp.concatenate([first[:, :rows], second[:, :rows]], axis=1)
+        out_ref[rows // 2 :, pl.ds(at, block)] = jnp.concatenate([first[:, rows:], second[:, rows:]], axis=1)
     for group in (cores, ys, zs):
         for copy in group.values():
             copy.wait_send()
@@ -292,8 +301,8 @@
             pltpu.VMEM((depth, own_rows, band), f32),
             pltpu.VMEM((depth, own_rows, band), f32),
             pltpu.VMEM((depth, own_rows, band), f32),
-            pltpu.VMEM((far, block, own_rows), f32),
-            pltpu.VMEM((2 * far, own_rows, own_rows), f32),
+            pltpu.VMEM((2 * far, own_rows // 2, block), f32),
+            pltpu.VMEM((2 * far, own_rows // 2, block), f32),
             dma((nblocks,)),
             dma((nblocks,)),
             dma((depth,)),

time: 58.8 us -> 55.4 us (0.942)
  Pallas kernels: 56.7 us -> 52.9 us
    pallas_call x1, Pallas kernels: 38.1 us -> 34.6 us  [body(): pl.pallas_call(functools.partial(scatter_kernel, shards, scale), out_shap...]
where the time goes in v4:
time: 55.4 us; the launch traced here: 55.1 us
  Pallas kernels  52.9 us (95%)
  local copies, waits for them, and re-layouts  1.48 us (3%)
  between operations  0.68 us (1%)
    pallas_call x1, Pallas kernels, body(): pl.pallas_call(functools.partial(scatter_kernel, shards, scale), out_shap...  34.6 us
    pallas_call x1, Pallas kernels, body(): pl.pallas_call(functools.partial(gather_kernel, shards), out_shape=pltpu....  13.3 us
    pallas_call x1, Pallas kernels, body(): pl.pallas_call(functools.partial(partial_kernel, shards, scale, own), out...  5.03 us
    unnamed x3, local copies, waits for them, and re-layouts  1.48 us

profile of v4, /device:TPU:0, one launch (start us, length us, event | category | flops | bytes accessed | tf_op | source)
XLA Modules:
  0.0 55.1 jit_solution(5744848596164102316)
XLA Ops:
  0.7 13.3 %shard_map.64.coeff_ref = bf16[1024,256]{1,0:T(8,128)(2,1)S(1)} custom-call(bf16[64,256]{1,0:T(8,128)(2,1)} %coeff_ref.1), custom_call_target="tpu_custom_call" | custom-call | tf_op jit(solution)/shard_map/pallas_call | solution.py:256
  13.9 0.0 copy-start
  13.9 0.8 %copy-done = bf16[1024,256]{1,0:T(8,128)(2,1)} copy-done((bf16[1024,256]{1,0:T(8,128)(2,1)}, bf16[1024,256]{1,0:T(8,128)(2,1)S(1)}, u32[]{:S(2)}) %copy-start) | copy-done | bytes 524312
  14.7 5.0 %shard_map.65.half_ref = bf16[1536,2048]{1,0:T(8,128)(2,1)S(1)} custom-call(s32[8]{0:T(128)} %bitcast.4, s32[8]{0:T(128)} %bitcast.5, s32[1]{0:T(128)S(6)} %copy.8.count_in, s32[16]{0:T(128)} %owner_in.1, bf16[8,8,128,128]{3,2,1,0:T(8,128)(2,1)} %bitcast.3, bf16[1024,256]{1,0:T(8,128)(2,1)} %copy-done), custom_call_target="tpu_custom_call" | custom-call | tf_op jit(solution)/shard_map/pallas_call | solution.py:267
  19.8 34.6 %shard_map.66 = f32[64,1024]{1,0:T(8,128)S(1)} custom-call(bf16[1536,2048]{1,0:T(8,128)(2,1)S(1)} %shard_map.65.half_ref), custom_call_target="tpu_custom_call" | custom-call | tf_op jit(solution)/shard_map/pallas_call | solution.py:292
  54.3 0.7 %copy.9 = f32[64,1024]{1,0:T(8,128)} copy(f32[64,1024]{1,0:T(8,128)S(1)} %shard_map.66) | data formatting | bytes 524288
Async XLA Ops:
  13.9 0.8 %copy-start = (bf16[1024,256]{1,0:T(8,128)(2,1)}, bf16[1024,256]{1,0:T(8,128)(2,1)S(1)}, u32[]{:S(2)}) copy-start(bf16[1024,256]{1,0:T(8,128)(2,1)S(1)} %shard_map.64.coeff_ref) | copy-start | bytes 1572868

commit v5 on v4

--- a/solution.py
+++ b/solution.py
@@ -129,16 +129,17 @@
     met = greet(me, shards)
     out_ref[pl.ds(pl.multiple_of(me * rows, rows), rows), :] = coeff_ref[...]
     met()
-    copies = []
-    for k in range(1, chips):
+    copies = {}
+    near_first = sorted(range(1, chips), key=lambda k: min(k, chips - k))
+    for k in near_first[::-1]:
         target = lax.rem(chip + k, chips) * 2 + core
-        copies.append(push(coeff_ref, rows_of(me), send.at[k], recv.at[k], target))
+        copies[k] = push(coeff_ref, rows_of(me), send.at[k], recv.at[k], target)
     passed = [push(coeff_ref, rows_of(me), pass_send.at[0], pass_recv.at[0], sibling)]
-    for k in range(1, chips):
-        copies[k - 1].wait_recv()
+    for k in near_first:
+        copies[k].wait_recv()
         source = lax.rem(chip + chips - k, chips) * 2 + core
         passed.append(push(rows_of(source), rows_of(source), pass_send.at[k], pass_recv.at[k], sibling))
-    for copy in copies:
+    for copy in copies.values():
         copy.wait_send()
     for copy in passed:
         copy.wait()
@@ -193,18 +194,31 @@
     for k in offsets:
         multiply(k, 0)
     zs = {}
+    near = band // block
+    middle = (chips - near + 1) * block
+    pieces = ((block, middle), (0, block), (middle, band))
     for k in offsets:
         cores[k, 0].wait_recv()
         ys[k].wait_recv()
         held[k] = part_ref[2 * k, mine, :] + from_core[2 * k] + from_y[k]
         if k:
-            zs[k] = push(held.at[k], from_z.at[k], z_s.at[k], z_r.at[k], (lax.rem(z + k, depth) * 2 + y) * 2 + core)
-    for k in zs:
-        zs[k].wait_recv()
-        held[0] += from_z[k]
-
+            for i, (low, high) in enumerate(pieces):
+                zs[k, i] = push(
+                    held.at[k, :, low:high],
+                    from_z.at[k, :, low:high],
+                    z_s.at[3 * k + i],
+                    z_r.at[3 * k + i],
+                    (lax.rem(z + k, depth) * 2 + y) * 2 + core,
+                )
+
+    def gather_sums(i):
+        low, high = pieces[i]
+        for k in offsets[:-1]:
+            zs[k, i].wait_recv()
+            held[0, :, low:high] += from_z[k, :, low:high]
+
+    gather_sums(0)
     fars = []
-    near = band // block
     for k in range(1, chips - near + 1):
         flipped = held[0, :, k * block : (k + 1) * block].T
         for h in range(2):
@@ -222,6 +236,8 @@
                     lax.rem(chip + k, chips) * 2 + h,
                 )
             )
+    gather_sums(1)
+    gather_sums(2)
     for k in range(near):
         at = pl.multiple_of(lax.rem(chip + k, chips) * block, block)
         out_ref[:, pl.ds(at, block)] = held[0, :, k * block : (k + 1) * block]
@@ -307,8 +323,8 @@
             dma((nblocks,)),
             dma((depth,)),
             dma((depth,)),
-            dma((depth,)),
-            dma((depth,)),
+            dma((3 * depth,)),
+            dma((3 * depth,)),
             dma((2 * far,)),
             dma((2 * far,)),
         ],

time: 55.4 us -> 55.1 us (level)
    pallas_call x1, Pallas kernels: 13.3 us -> 14.6 us  [body(): pl.pallas_call(functools.partial(gather_kernel, shards), out_shape=pltpu....]
    pallas_call x1, Pallas kernels: 34.6 us -> 33.5 us  [body(): pl.pallas_call(functools.partial(scatter_kernel, shards, scale), out_shap...]
where the time goes in v5:
time: 55.1 us; the launch traced here: 55 us
  Pallas kernels  52.8 us (96%)
  local copies, waits for them, and re-layouts  1.48 us (3%)
  between operations  0.68 us (1%)
    pallas_call x1, Pallas kernels, body(): pl.pallas_call(functools.partial(scatter_kernel, shards, scale), out_shap...  33.5 us
    pallas_call x1, Pallas kernels, body(): pl.pallas_call(functools.partial(gather_kernel, shards), out_shape=pltpu....  14.6 us
    pallas_call x1, Pallas kernels, body(): pl.pallas_call(functools.partial(partial_kernel, shards, scale, own), out...  4.73 us
    unnamed x3, local copies, waits for them, and re-layouts  1.48 us

profile of v5, /device:TPU:0, one launch (start us, length us, event | category | flops | bytes accessed | tf_op | source)
XLA Modules:
  0.0 55.0 jit_solution(5757487494247594995)
XLA Ops:
  0.7 14.6 %shard_map.64.coeff_ref = bf16[1024,256]{1,0:T(8,128)(2,1)S(1)} custom-call(bf16[64,256]{1,0:T(8,128)(2,1)} %coeff_ref.1), custom_call_target="tpu_custom_call" | custom-call | tf_op jit(solution)/shard_map/pallas_call | solution.py:272
  15.3 0.0 copy-start
  15.3 0.8 %copy-done = bf16[1024,256]{1,0:T(8,128)(2,1)} copy-done((bf16[1024,256]{1,0:T(8,128)(2,1)}, bf16[1024,256]{1,0:T(8,128)(2,1)S(1)}, u32[]{:S(2)}) %copy-start) | copy-done | bytes 524312
  16.1 4.7 %shard_map.65.half_ref = bf16[1536,2048]{1,0:T(8,128)(2,1)S(1)} custom-call(s32[8]{0:T(128)} %bitcast.4, s32[8]{0:T(128)} %bitcast.5, s32[1]{0:T(128)S(6)} %copy.8.count_in, s32[16]{0:T(128)} %owner_in.1, bf16[8,8,128,128]{3,2,1,0:T(8,128)(2,1)} %bitcast.3, bf16[1024,256]{1,0:T(8,128)(2,1)} %copy-done), custom_call_target="tpu_custom_call" | custom-call | tf_op jit(solution)/shard_map/pallas_call | solution.py:283
  20.8 33.5 %shard_map.66 = f32[64,1024]{1,0:T(8,128)S(1)} custom-call(bf16[1536,2048]{1,0:T(8,128)(2,1)S(1)} %shard_map.65.half_ref), custom_call_target="tpu_custom_call" | custom-call | tf_op jit(solution)/shard_map/pallas_call | solution.py:308
  54.3 0.7 %copy.9 = f32[64,1024]{1,0:T(8,128)} copy(f32[64,1024]{1,0:T(8,128)S(1)} %shard_map.66) | data formatting | bytes 524288
Async XLA Ops:
  15.3 0.8 %copy-start = (bf16[1024,256]{1,0:T(8,128)(2,1)}, bf16[1024,256]{1,0:T(8,128)(2,1)S(1)}, u32[]{:S(2)}) copy-start(bf16[1024,256]{1,0:T(8,128)(2,1)S(1)} %shard_map.64.coeff_ref) | copy-start | bytes 1572868

commit v6 on v5

--- a/solution.py
+++ b/solution.py
@@ -29,7 +29,7 @@
     ]
     for move in moves:
         move.start()
-    for move in moves:
+    for move in moves[:4]:
         move.wait()
     slots, aux_local, block, _ = tiles_ref.shape
     nbasis, occupied = coeff_ref.shape
@@ -40,6 +40,8 @@
     @pl.loop(0, shards)
     def _(d):
         place[owner_ref[d]] = d
+
+    moves[4].wait()
 
     @pl.loop(0, nblocks)
     def _(b):
@@ -75,17 +77,23 @@
             @pl.when(seen > 0)
             def _():
                 for p in range(aux_local):
-                    half[pl.ds(where, rows), p * occupied : (p + 1) * occupied] = total[
-                        p * block + piece * rows : p * block + (piece + 1) * rows, :
-                    ].astype(jnp.bfloat16).astype(half.dtype)
+                    value = total[p * block + piece * rows : p * block + (piece + 1) * rows, :]
+                    half[pl.ds(where, rows), p * occupied : (p + 1) * occupied] = value.astype(
+                        jnp.bfloat16
+                    ).astype(half.dtype)
 
             @pl.when(seen == 0)
             def _():
                 half[pl.ds(where, rows), :] = jnp.zeros((rows, aux_local * occupied), half.dtype)
 
-    if own:
-        half[nbasis:, :] = half[: half.shape[0] - nbasis, :]
-    else:
+            if own:
+
+                @pl.when(where < half.shape[0] - nbasis)
+                def _():
+                    again = pl.multiple_of(where + nbasis, rows)
+                    half[pl.ds(again, rows), :] = half[pl.ds(where, rows), :]
+
+    if not own:
 
         @pl.loop(0, nblocks)
         def _(d):

time: 55.1 us -> 55 us (level)
    pallas_call x1, Pallas kernels: 33.5 us -> 32.3 us  [body(): pl.pallas_call(functools.partial(scatter_kernel, shards, scale), out_shap...]
    pallas_call x1, Pallas kernels: 4.73 us -> 5.44 us  [body(): pl.pallas_call(functools.partial(partial_kernel, shards, scale, own), out...]
where the time goes in v6:
time: 55 us; the launch traced here: 54.6 us
  Pallas kernels  52.4 us (95%)
  local copies, waits for them, and re-layouts  1.48 us (3%)
  between operations  0.68 us (1%)
    pallas_call x1, Pallas kernels, body(): pl.pallas_call(functools.partial(scatter_kernel, shards, scale), out_shap...  32.3 us
    pallas_call x1, Pallas kernels, body(): pl.pallas_call(functools.partial(gather_kernel, shards), out_shape=pltpu....  14.6 us
    pallas_call x1, Pallas kernels, body(): pl.pallas_call(functools.partial(partial_kernel, shards, scale, own), out...  5.44 us
    unnamed x3, local copies, waits for them, and re-layouts  1.48 us

profile of v6, /device:TPU:0, one launch (start us, length us, event | category | flops | bytes accessed | tf_op | source)
XLA Modules:
  0.0 54.6 jit_solution(17478246217510896585)
XLA Ops:
  0.7 14.6 %shard_map.64.coeff_ref = bf16[1024,256]{1,0:T(8,128)(2,1)S(1)} custom-call(bf16[64,256]{1,0:T(8,128)(2,1)} %coeff_ref.1), custom_call_target="tpu_custom_call" | custom-call | tf_op jit(solution)/shard_map/pallas_call | solution.py:280
  15.3 0.0 copy-start
  15.3 0.8 %copy-done = bf16[1024,256]{1,0:T(8,128)(2,1)} copy-done((bf16[1024,256]{1,0:T(8,128)(2,1)}, bf16[1024,256]{1,0:T(8,128)(2,1)S(1)}, u32[]{:S(2)}) %copy-start) | copy-done | bytes 524312
  16.1 5.4 %shard_map.65.half_ref = bf16[1536,2048]{1,0:T(8,128)(2,1)S(1)} custom-call(s32[8]{0:T(128)} %bitcast.4, s32[8]{0:T(128)} %bitcast.5, s32[1]{0:T(128)S(6)} %copy.8.count_in, s32[16]{0:T(128)} %owner_in.1, bf16[8,8,128,128]{3,2,1,0:T(8,128)(2,1)} %bitcast.3, bf16[1024,256]{1,0:T(8,128)(2,1)} %copy-done), custom_call_target="tpu_custom_call" | custom-call | tf_op jit(solution)/shard_map/pallas_call | solution.py:291
  21.5 32.3 %shard_map.66 = f32[64,1024]{1,0:T(8,128)S(1)} custom-call(bf16[1536,2048]{1,0:T(8,128)(2,1)S(1)} %shard_map.65.half_ref), custom_call_target="tpu_custom_call" | custom-call | tf_op jit(solution)/shard_map/pallas_call | solution.py:316
  53.8 0.7 %copy.9 = f32[64,1024]{1,0:T(8,128)} copy(f32[64,1024]{1,0:T(8,128)S(1)} %shard_map.66) | data formatting | bytes 524288
Async XLA Ops:
  15.3 0.8 %copy-start = (bf16[1024,256]{1,0:T(8,128)(2,1)}, bf16[1024,256]{1,0:T(8,128)(2,1)S(1)}, u32[]{:S(2)}) copy-start(bf16[1024,256]{1,0:T(8,128)(2,1)S(1)} %shard_map.64.coeff_ref) | copy-start | bytes 1572868
